TPU v7x, 32 devices: a whole 2x2x4 slice. The times are simulated.
32 devices in a mesh: slab: 16 (over z, y, x), batch: 2 (over core).
Axes of the slice: x: 2, y: 2, z: 4, core: 2. Of those that a mesh axis runs over, the one named last changes fastest.
Arguments:
- field: bfloat16 [2, 16, 128, 256, 128], P('batch', None, 'slab'), may hold values from -6 to 6
- cotangent: bfloat16 [2, 16, 128, 256, 128], P('batch', None, 'slab'), may hold values from -6 to 6
- spectral_weight: bfloat16 [1024, 2, 16, 512], P('slab'), may hold values from -1 to 1
- point_weight: bfloat16 [16, 16], replicated, may hold values from -1.5 to 1.5
- point_bias: float32 [16], replicated, may hold values from -3 to 3
Outputs:
- input_grad: bfloat16 [2, 16, 128, 256, 128], P('batch', None, 'slab')
- grad_spec: float32 [1024, 2, 16, 512], P('slab')
- grad_point: float32 [16, 16], replicated
- grad_bias: float32 [16], replicated
All inputs are finite; a program needn't handle non-finite values.
Results may differ from a plain program's by a relative error of at most 0.018.
Values may be sent and summed in bfloat16 or wider, within the bound.
A program may use at most 192 MiB of HBM per device.

v0:
```python
import math

import jax
import jax.numpy as jnp
from jax import lax
from jax.sharding import PartitionSpec as P

MX = 32
MY = 32
MZ = 32


def half_einsum(form, left, right):
    return jnp.einsum(form, left, right, preferred_element_type=jnp.float32)


def mode_freqs(number, length):
    indices = jnp.arange(number, dtype=jnp.int32)
    return jnp.where(indices < number // 2, indices, indices + (length - number))


def phase_grid(positions, frequencies, length):
    product = positions[:, None] * frequencies[None, :] % length
    return product.astype(jnp.float32) * (2.0 * math.pi / length)


def rotation(phases, orient):
    cosine = jnp.cos(phases)
    sine_part = orient * jnp.sin(phases)
    upper = jnp.stack([cosine, -sine_part], axis=1)
    lower = jnp.stack([sine_part, cosine], axis=1)
    return jnp.stack([upper, lower], axis=0).astype(jnp.bfloat16)


def plane_tables(rows_y, rows_z):
    phase_y = phase_grid(jnp.arange(rows_y, dtype=jnp.int32), mode_freqs(MY, rows_y), rows_y)
    phase_z = phase_grid(
        jnp.arange(rows_z, dtype=jnp.int32), jnp.arange(MZ, dtype=jnp.int32), rows_z
    )
    forward_y = jnp.stack([jnp.cos(phase_y), -jnp.sin(phase_y)], axis=1).astype(jnp.bfloat16)
    forward_z = rotation(phase_z, 1.0)
    inverse_z = rotation(phase_z.T, -1.0)
    inverse_y = jnp.stack([jnp.cos(phase_y).T, -jnp.sin(phase_y).T], axis=0).astype(jnp.bfloat16)
    return (forward_y, forward_z, inverse_z, inverse_y)


def yz_forward(slab_data, tables):
    partial_value = half_einsum("bcxyz,yrm->bcxrmz", slab_data, tables[0]).astype(jnp.bfloat16)
    spectrum = half_einsum("bcxrmz,rzsk->bcxsmk", partial_value, tables[1]).astype(jnp.bfloat16)
    return spectrum.reshape(spectrum.shape[:4] + (MY * MZ,))


def yz_inverse(planes_in, tables, factor):
    shaped = planes_in.reshape(planes_in.shape[:4] + (MY, MZ))
    rolled = half_einsum("boxsmk,skrz->boxrmz", shaped, tables[2]).astype(jnp.bfloat16)
    return factor * half_einsum("boxrmz,rmy->boxyz", rolled, tables[3])


def mix_modes(spectrum, weights_f):

    def apply(values, weight_part):
        return jnp.einsum("biap,pioa->boap", values, weight_part, precision=lax.Precision.HIGHEST)

    real_part, imag_part = (spectrum[:, :, 0], spectrum[:, :, 1])
    first = apply(real_part, weights_f[:, 0]) - apply(imag_part, weights_f[:, 1])
    second = apply(real_part, weights_f[:, 1]) + apply(imag_part, weights_f[:, 0])
    return jnp.stack([first, second], axis=2)


def adjoint_mix(spectrum, weights_f):

    def apply(values, weight_part):
        return jnp.einsum("boap,pioa->biap", values, weight_part, precision=lax.Precision.HIGHEST)

    real_part, imag_part = (spectrum[:, :, 0], spectrum[:, :, 1])
    first = apply(real_part, weights_f[:, 0]) + apply(imag_part, weights_f[:, 1])
    second = apply(imag_part, weights_f[:, 0]) - apply(real_part, weights_f[:, 1])
    return jnp.stack([first, second], axis=2)


def weight_grad(modes_in, modes_out):

    def apply(left, right):
        return jnp.einsum("biap,boap->pioa", left, right, precision=lax.Precision.HIGHEST)

    first = apply(modes_in[:, :, 0], modes_out[:, :, 0]) + apply(
        modes_in[:, :, 1], modes_out[:, :, 1]
    )
    second = apply(modes_in[:, :, 0], modes_out[:, :, 1]) - apply(
        modes_in[:, :, 1], modes_out[:, :, 0]
    )
    stacked = jnp.stack([first, second], axis=1)
    return stacked.reshape(
        stacked.shape[0], 2, stacked.shape[2], stacked.shape[3] * stacked.shape[4]
    )


def activation_grad(pre, upstream):
    _, pull = jax.vjp(lambda values: jax.nn.gelu(values, approximate=True), pre)
    return pull(upstream)[0]


def body(field, cotangent, spectral_weight, point_weight, point_bias):
    samples, channels, planes, rows_y, rows_z = field.shape
    total_x = planes * lax.axis_size("slab")
    total_samples = samples * lax.axis_size("batch")
    tables = plane_tables(rows_y, rows_z)
    freq_x = mode_freqs(MX, total_x)
    local_x = lax.axis_index("slab") * planes + jnp.arange(planes, dtype=jnp.int32)
    phase_local = phase_grid(local_x, freq_x, total_x)
    cells = total_x * rows_y * rows_z
    scale_f = 1.0 / math.sqrt(cells)
    scale_i = 1.0 / math.sqrt(MX * MY * MZ)
    scale_p = 1.0 / math.sqrt(total_samples * cells)
    scale_w = math.sqrt(MX * MY * MZ / (total_samples * cells))
    weights_f = spectral_weight.astype(jnp.float32).reshape(
        spectral_weight.shape[0], 2, channels, channels, MX
    )

    def to_modes(spectrum, factor):
        partial_value = factor * half_einsum(
            "bcxrp,rxsa->bcsap", spectrum, rotation(phase_local, 1.0)
        )
        return lax.psum_scatter(partial_value, "slab", scatter_dimension=4, tiled=True)

    def to_slabs(spectrum):
        table_local = rotation(phase_local.T, -1.0)
        return half_einsum(
            "bosap,sarx->boxrp", lax.all_gather(spectrum, "slab", axis=4, tiled=True), table_local
        ).astype(jnp.bfloat16)

    modes_u = to_modes(yz_forward(field, tables), scale_f)
    mixed = mix_modes(modes_u, weights_f).astype(jnp.bfloat16)
    back_v = to_slabs(mixed)
    pre = yz_inverse(back_v, tables, scale_i) + half_einsum("bixyz,io->boxyz", field, point_weight)
    pre = pre + point_bias[None, :, None, None, None]
    dpre = activation_grad(pre, cotangent.astype(jnp.float32)).astype(jnp.bfloat16)
    point_local = half_einsum("bixyz,boxyz->io", field, dpre)
    bias_local = jnp.sum(dpre.astype(jnp.float32), axis=(0, 2, 3, 4))
    point_total, bias_total = lax.psum((point_local, bias_local), ("slab", "batch"))
    modes_d = to_modes(yz_forward(dpre, tables), scale_i)
    spec_total = lax.psum(weight_grad(modes_u, modes_d).astype(jnp.bfloat16), "batch").astype(
        jnp.float32
    )
    back_d = to_slabs(adjoint_mix(modes_d, weights_f).astype(jnp.bfloat16))
    input_grad = yz_inverse(back_d, tables, scale_f) + half_einsum(
        "boxyz,io->bixyz", dpre, point_weight
    )
    return (
        input_grad.astype(jnp.bfloat16),
        scale_w * spec_total,
        scale_p * point_total,
        scale_p * bias_total,
    )


def solution(mesh):
    placed = (
        P("batch", None, "slab", None, None),
        P("batch", None, "slab", None, None),
        P("slab", None, None, None),
        P(),
        P(),
    )
    return jax.shard_map(
        body,
        mesh=mesh,
        in_specs=placed,
        out_specs=(P("batch", None, "slab", None, None), P("slab", None, None, None), P(), P()),
        check_vma=False,
    )
```

profile of v0, /device:TPU:0, one launch (start us, length us, event | category | flops | bytes accessed | tf_op | source)
XLA Modules:
  0.0 623.7 jit_solution(8318663621557097161)
XLA Ops:
  7.4 0.2 cosine_convert_fusion
  7.7 5.0 convert_bitcast_fusion.1
  12.7 3.1 fusion.55
  15.8 3.0 copy.58
  18.8 2.3 reshape.950
  21.3 2.8 fusion.36
  24.1 14.4 %copy.161 = f32[1,16,2,32,1024]{3,1,2,0,4:T(8,128)} copy(f32[1,16,2,32,1024]{4,3,1,2,0:T(8,128)} %fusion.36) | data formatting | bytes 8388608
  38.5 13.7 %reshape.991 = f32[1024,1024]{1,0:T(8,128)} reshape(f32[1024,1,2,16,32]{4,3,2,1,0:T(8,128)} %bitcast.415) | data formatting | bytes 8388608
  52.2 1.5 copy-done.1
  53.7 3.8 copy.59
  57.6 92.6 %reduce-scatter.7.cloned.1.call-done = f32[64,1024]{1,0:T(8,128)} async-done(((f32[1024,1024]{1,0:T(8,128)}), f32[64,1024]{1,0:T(8,128)}) %reduce-scatter.7.cloned.1.call-update) | async-done | bytes 262160
  150.1 1.3 reshape.992
  151.4 1.0 fusion.149
  152.4 0.3 copy.169
  152.7 0.3 copy.170
  152.9 3.7 fusion.29
  156.6 0.3 copy.97
  156.9 0.3 copy.113
  157.2 0.3 copy.105
  157.5 0.3 copy.89
  157.9 0.9 pad_maximum_fusion.1
  159.2 0.2 cosine_convert_fusion.1
  159.5 12.3 %fusion.25 = f32[16,8,256,128]{3,0,2,1:T(8,128)} fusion(bf16[16,8,256,128]{3,2,1,0:T(8,128)(2,1)} %bitcast.419, bf16[16,16]{1,0:T(8,128)(2,1)S(1)} %copy-done), kind=kOutput, calls=%fused_computation.33 | convolution fusion | flops 134217728 | bytes 25166336 | tf_op jit(solution)/shard_map/bixyz,io->boxyz/dot_general | solution.py:14
  171.8 99.6 %all-gather.3.cloned.1.call-done = bf16[1,16,2,32,1024]{3,1,2,0,4:T(8,128)(2,1)} async-done(((bf16[1,16,2,32,64]{3,1,2,0,4:T(8,128)(2,1)}), bf16[1,16,2,32,1024]{3,1,2,0,4:T(8,128)(2,1)}) %all-gather.3.cloned.1.call-update) | async-done | bytes 2097168 | tf_op jit(solution)/shard_map/all_gather | solution.py:129
  271.4 8.3 %copy.60 = bf16[1,16,2,32,1024]{4,3,2,1,0:T(8,128)(2,1)S(1)} copy(bf16[1,16,2,32,1024]{3,1,2,0,4:T(8,128)(2,1)} %all-gather.3.cloned.1.call-done) | data formatting | bytes 4194304 | tf_op jit(solution)/shard_map/all_gather | solution.py:129
  279.7 0.4 fusion.81
  280.2 1.6 reshape.934
  281.8 21.4 %convert_reduce_fusion = (f32[16]{0:T(128)S(1)}, bf16[1,16,8,256,128]{4,3,2,1,0:T(8,128)(2,1)}) fusion(f32[16]{0:T(128)S(1)} %copy-done.3, f32[16,8,256,128]{3,0,2,1:T(8,128)} %fusion.25, bf16[16,8,2,32,32]{4,3,1,0,2:T(8,128)(2,1)S(1)} %reshape.934, bf16[1,32,2,128]{3,1,0,2:T(8,128)(2,1)S(1)} %get-tuple-element.41, ...), kind=kOutput, calls=%fused_computation.22 | convolution fusion | flops 781320192 | bytes 34144384 | tf_op jit(solution)/shard_map/boxrmz,rmy->boxyz/dot_general | solution.py:14
  303.1 5.0 convert_bitcast_fusion
  308.1 3.1 fusion.58
  311.3 3.2 copy.67
  314.5 2.3 reshape.972
  316.9 2.8 fusion.35
  319.6 14.4 %copy.163 = f32[1,16,2,32,1024]{3,1,2,0,4:T(8,128)} copy(f32[1,16,2,32,1024]{4,3,1,2,0:T(8,128)} %fusion.35) | data formatting | bytes 8388608
  334.0 13.7 %reshape.993 = f32[1024,1024]{1,0:T(8,128)} reshape(f32[1024,1,2,16,32]{4,3,2,1,0:T(8,128)} %bitcast.416) | data formatting | bytes 8388608
  347.7 1.0 copy-done.2
  348.7 0.3 copy.165
  348.9 1.0 copy.166
  349.9 91.2 %reduce-scatter.9.cloned.1.call-done = f32[64,1024]{1,0:T(8,128)} async-done(((f32[1024,1024]{1,0:T(8,128)}), f32[64,1024]{1,0:T(8,128)}) %reduce-scatter.9.cloned.1.call-update) | async-done | bytes 262160
  441.2 1.3 reshape.994
  442.6 0.3 copy.167
  442.9 0.3 copy.168
  443.1 2.1 add_convert_fusion
  445.3 3.0 pad_maximum_fusion
  448.3 0.3 copy.171
  448.6 0.3 copy.172
  448.8 4.3 fusion.33
  453.2 0.3 copy.138
  453.4 0.3 copy.146
  453.7 0.3 copy.154
  454.0 0.3 copy.130
  454.5 1.0 pad_maximum_fusion.2
  455.5 16.4 %fusion.87 = f32[16,16]{0,1:T(8,128)S(1)} fusion(bf16[16,8,256,128]{3,2,1,0:T(8,128)(2,1)} %bitcast.420, bf16[16,8,256,128]{3,2,1,0:T(8,128)(2,1)} %bitcast.421), kind=kOutput, calls=%fused_computation.86 | convolution fusion | flops 134217728 | bytes 16778240 | tf_op jit(solution)/shard_map/bixyz,boxyz->io/dot_general | solution.py:14
  471.8 39.7 %all-reduce = (f32[16,16]{0,1:T(8,128)S(1)}, f32[16]{0:T(128)S(1)}) all-reduce(f32[16,16]{0,1:T(8,128)S(1)} %fusion.87, f32[16]{0:T(128)S(1)} %get-tuple-element.58), channel_id=1, replica_groups=mesh['slab'=16,'batch'=2] {'slab','batch'}, use_global_device_ids=true, to_apply=%region_3.4 | all-reduce | flops 272 | bytes 2176 | tf_op jit(solution)/shard_map/psum | solution.py:140
  511.6 0.7 copy.76
  512.2 0.5 broadcast_multiply_fusion.1
  512.8 14.2 %fusion.22 = f32[8,256,128,16]{2,3,1,0:T(8,128)} fusion(bf16[16,8,256,128]{3,2,1,0:T(8,128)(2,1)} %bitcast.422, bf16[16,16]{1,0:T(8,128)(2,1)S(1)} %copy-done), kind=kOutput, calls=%fused_computation.30 | convolution fusion | flops 134217728 | bytes 25166336 | tf_op jit(solution)/shard_map/boxyz,io->bixyz/dot_general | solution.py:14
  526.9 6.6 %convert_multiply_fusion.2 = f32[64,2,16,512]{0,3,2,1:T(8,128)} fusion(bf16[64,2,16,512]{0,3,2,1:T(8,128)(2,1)} %all-reduce.3.cloned.1.call-done), kind=kLoop, calls=%fused_computation.27 | loop fusion | flops 2097152 | bytes 6291456 | tf_op jit(solution)/shard_map/mul | solution.py:151
  533.6 7.3 %copy.75 = f32[64,2,16,512]{3,2,1,0:T(8,128)} copy(f32[64,2,16,512]{0,3,2,1:T(8,128)} %convert_multiply_fusion.2) | data formatting | bytes 8388608
  540.9 53.0 %all-gather.5.cloned.1.call-done = bf16[1,16,2,32,1024]{3,1,2,0,4:T(8,128)(2,1)} async-done(((bf16[1,16,2,32,64]{3,1,2,0,4:T(8,128)(2,1)}), bf16[1,16,2,32,1024]{3,1,2,0,4:T(8,128)(2,1)}) %all-gather.5.cloned.1.call-update) | async-done | bytes 2097168 | tf_op jit(solution)/shard_map/all_gather | solution.py:129
  593.9 8.3 %copy.68 = bf16[1,16,2,32,1024]{4,3,2,1,0:T(8,128)(2,1)S(1)} copy(bf16[1,16,2,32,1024]{3,1,2,0,4:T(8,128)(2,1)} %all-gather.5.cloned.1.call-done) | data formatting | bytes 4194304 | tf_op jit(solution)/shard_map/all_gather | solution.py:129
  602.2 0.4 fusion.84
  602.6 1.6 reshape.942
  604.2 12.8 %fusion.12 = bf16[1,16,8,256,128]{4,3,2,1,0:T(8,128)(2,1)} fusion(f32[8,256,128,16]{2,3,1,0:T(8,128)} %fusion.22, bf16[16,8,2,32,32]{4,3,1,0,2:T(8,128)(2,1)S(1)} %reshape.942, bf16[1,32,2,128]{3,1,0,2:T(8,128)(2,1)S(1)} %get-tuple-element.41, bf16[1,32,2,128]{3,1,0,2:T(8,128)(2,1)S(1)} %get-tuple-element.40, ...), kind=kOutput, calls=%fused_computation.17 | convolution fusion | flops 684851200 | bytes 25755648 | tf_op jit(solution)/shard_map/boxrmz,rmy->boxyz/dot_general | solution.py:14
  (36 shorter events, 1.4 us)
Async XLA Ops:
  7.2 152.3 %copy-start = (bf16[16,16]{1,0:T(8,128)(2,1)S(1)}, bf16[16,16]{1,0:T(8,128)(2,1)}, u32[]{:S(2)}) copy-start(bf16[16,16]{1,0:T(8,128)(2,1)} %param.8) | copy-start | bytes 1540
  7.2 143.0 %reduce-scatter.7.cloned.1.call-start = ((), (), s32[]{:S(2)}) async-start(), calls=%async_computation.5 | async-start | bytes 4456448
  52.1 1.6 copy-start.1
  52.2 219.3 %all-gather.3.cloned.1.call-start = ((), (), s32[]{:S(2)}) async-start(), calls=%async_computation.2 | async-start | bytes 8912896 | tf_op jit(solution)/shard_map/all_gather | solution.py:129
  158.8 282.3 %reduce-scatter.9.cloned.1.call-start = ((), (), s32[]{:S(2)}) async-start(), calls=%async_computation.6 | async-start | bytes 4456448
  279.7 2.1 copy-start.3
  347.6 1.0 copy-start.2
  347.7 179.3 %all-reduce.3.cloned.1.call-start = ((), (), s32[]{:S(2)}) async-start(), calls=%async_computation.4 | async-start | bytes 8388608 | tf_op jit(solution)/shard_map/psum | solution.py:142
  448.3 145.6 %all-gather.5.cloned.1.call-start = ((), (), s32[]{:S(2)}) async-start(), calls=%async_computation.3 | async-start | bytes 8912896 | tf_op jit(solution)/shard_map/all_gather | solution.py:129
Sparse Core Ops, SparseCore 0:
  52.3 97.8 reduce-scatter.6
  159.0 112.4 all-gather.2
  347.8 93.3 reduce-scatter.8
  448.4 28.0 all-reduce.2
  479.4 114.4 all-gather.4
where the time goes:
time: 634 us; the launch traced here: 624 us
  waiting for transfers between devices  337 us (53%)
  local copies, waits for them, and re-layouts  110 us (17%)
  matrix products  99.7 us (16%)
  blocking collectives  39.7 us (6%)
  other arithmetic  23.4 us (4%)
  between operations  14.3 us (2%)
    unnamed x7, waiting for transfers between devices  184 us
    all_gather x2, waiting for transfers between devices, to_slabs(): lax.all_gather(spectrum, 'slab', axis=4, tiled=True)  153 us
    dot_general x13, matrix products, half_einsum(): return jnp.einsum(form, left, right, preferred_element_type=jnp.float32)  99.7 us
    unnamed x25, local copies, waits for them, and re-layouts  75.7 us
    psum x1, blocking collectives, body(): lax.psum((point_local, bias_local), ('slab', 'batch'))  39.7 us
    all_gather x2, local copies, waits for them, and re-layouts, to_slabs(): lax.all_gather(spectrum, 'slab', axis=4, tiled=True)  16.6 us
  transfers between devices with their start and end apart: 5, of which 4 were waited for; matrix products, arithmetic and copies ran while one was open for 11% of the time, Pallas kernels for 0%

commit v1 on v0

v1 whole, which is shorter than its diff:
```python
import functools
import math

import jax
import jax.numpy as jnp
import ml_dtypes
import numpy as np
from jax import lax
from jax.experimental import pallas as pl
from jax.experimental.pallas import tpu as pltpu
from jax.sharding import PartitionSpec as P

MX = 32
MY = 32
MZ = 32
PB = 8
BF = jnp.bfloat16
F32 = jnp.float32
MESH = pl.DeviceIdType.MESH
VMEM = pl.BlockSpec(memory_space=pltpu.VMEM)


def np_freqs(number, length):
    indices = np.arange(number)
    return np.where(indices < number // 2, indices, indices + (length - number))


def np_phase(positions, frequencies, length):
    product = positions[:, None] * frequencies[None, :] % length
    return product.astype(np.float64) * (2.0 * math.pi / length)


def x_tables(n, planes, channels):
    total = n * planes
    phase = np_phase(np.arange(total), np_freqs(MX, total), total)
    cosine, sine = np.cos(phase), np.sin(phase)
    forward = np.stack(
        [np.stack([cosine, -sine], axis=1), np.stack([sine, cosine], axis=1)], axis=0
    )
    inverse = np.stack(
        [np.stack([cosine, -sine], axis=1), np.stack([sine, cosine], axis=1)], axis=0
    )

    def rows(table, copies):
        table = table.reshape(2, n, planes, 2, MX).transpose(1, 0, 2, 3, 4)
        table = table.reshape(n * 2 * planes, 2, 1, MX)
        table = np.broadcast_to(table, (table.shape[0], 2, copies, MX))
        return table.reshape(table.shape[0], 2 * copies * MX).astype(ml_dtypes.bfloat16)

    return jnp.asarray(rows(forward, channels)), jnp.asarray(rows(inverse, 4))


def enter(n, me, bat):
    barrier = pltpu.get_barrier_semaphore()

    def greet(k, carry):
        pl.semaphore_signal(
            barrier, inc=1, device_id={"slab": lax.rem(me + k, n)}, device_id_type=MESH
        )
        return carry

    lax.fori_loop(1, n, greet, 0)
    pl.semaphore_signal(barrier, inc=1, device_id={"batch": 1 - bat}, device_id_type=MESH)
    pl.semaphore_wait(barrier, n)


def peer_copy(n, me, k, source, target, landed, sems):
    to = lax.rem(me + k, n)
    return pltpu.make_async_remote_copy(
        src_ref=source(to),
        dst_ref=target(landed),
        send_sem=sems.at[0, k],
        recv_sem=sems.at[1, k],
        device_id={"slab": to},
        device_id_type=MESH,
    )


def send_all(n, me, source, target, sems):
    def step(k, carry):
        peer_copy(n, me, k, source, target, me, sems).start()
        return carry

    lax.fori_loop(1, n, step, 0)


def wait_all(n, me, source, target, sems):
    def step(k, carry):
        peer_copy(n, me, k, source, target, lax.rem(me - k + n, n), sems).wait()
        return carry

    lax.fori_loop(1, n, step, 0)


def expand(planes_ref, slot, block, table_ref):
    rows = planes_ref.shape[1] * planes_ref.shape[2]
    lanes = pl.ds(pl.multiple_of(block * (PB * 16), 128), PB * 16)
    part = planes_ref[slot, :, :, lanes].reshape(rows, PB * 16)
    both = lax.dot_general(
        part, table_ref[...], (((0,), (0,)), ((), ())), preferred_element_type=F32
    )
    half = both.shape[1] // 2
    return (
        both[:, :half].reshape(PB, 16, half),
        both[:, half:].reshape(PB, 16, half),
    )


def own_mask(channels):
    shape = (channels, channels * MX)
    row = lax.broadcasted_iota(jnp.int32, shape, 0)
    col = lax.broadcasted_iota(jnp.int32, shape, 1)
    low = row * MX
    return jnp.where((col >= low) & (col < low + MX), 1.0, 0.0).astype(F32)


def lane_fold(values):
    quarter = values.shape[-1] // 4
    return (
        values[..., :quarter]
        + values[..., quarter : 2 * quarter]
        + values[..., 2 * quarter : 3 * quarter]
        + values[..., 3 * quarter :]
    )


def contract(first, second, table_ref, out_ref, block):
    both = jnp.concatenate([lane_fold(first), lane_fold(second)], axis=-1)
    both = both.reshape(PB * 16, both.shape[-1]).astype(BF)
    result = lax.dot_general(
        table_ref[...], both, (((1,), (1,)), ((), ())), preferred_element_type=F32
    )
    lanes = pl.ds(pl.multiple_of(block * (PB * 16), 128), PB * 16)
    out_ref[:, :, lanes] = result.astype(BF).reshape(out_ref.shape[0], out_ref.shape[1], PB * 16)


def weight_pair(w_ref, block):
    at = pl.ds(block * PB, PB)
    return w_ref[at, 0].astype(F32), w_ref[at, 1].astype(F32)


def mix_forward(n, scale, s1, w, t, ti, r1, r2, s2, sems, pair):
    me = lax.axis_index("slab")
    bat = lax.axis_index("batch")
    enter(n, me, bat)
    one = (lambda to: s1.at[to], lambda at: r1.at[bat, at], sems.at[0])
    two = (lambda to: s2.at[to], lambda at: r2.at[at], sems.at[1])
    send_all(n, me, *one)
    r1[bat, me] = s1[me]
    wait_all(n, me, *one)
    cross = pltpu.make_async_remote_copy(
        src_ref=r1.at[bat],
        dst_ref=r1.at[bat],
        send_sem=pair.at[0],
        recv_sem=pair.at[1],
        device_id={"batch": 1 - bat},
        device_id_type=MESH,
    )
    cross.start()
    mask = own_mask(16)[None]

    def step(block, carry):
        u0, u1 = expand(r1, bat, block, t)
        u0, u1 = u0 * scale, u1 * scale
        w0, w1 = weight_pair(w, block)
        v0 = jnp.sum(u0 * w0 - u1 * w1, axis=1, keepdims=True) * mask
        v1 = jnp.sum(u0 * w1 + u1 * w0, axis=1, keepdims=True) * mask
        contract(v0, v1, ti, s2, block)
        return carry

    lax.fori_loop(0, w.shape[0] // PB, step, 0)
    send_all(n, me, *two)
    r2[me] = s2[me]
    cross.wait()
    wait_all(n, me, *two)


def mix_backward(
    n, scale_f, scale_i, scale_w, s3, part, w, t, ti, r1, grad, r4, total,
    r3, s4, slots, half, sems, pair,
):
    me = lax.axis_index("slab")
    bat = lax.axis_index("batch")
    enter(n, me, bat)
    one = (lambda to: s3.at[to], lambda at: r3.at[bat, at], sems.at[0])
    two = (lambda to: s4.at[to], lambda at: r4.at[at], sems.at[1])
    small = (lambda to: part, lambda at: slots.at[at], sems.at[2])
    send_all(n, me, *one)
    send_all(n, me, *small)
    r3[bat, me] = s3[me]
    slots[me] = part[...]
    wait_all(n, me, *one)

    def across(source, target, at):
        return pltpu.make_async_remote_copy(
            src_ref=source,
            dst_ref=target,
            send_sem=pair.at[2 * at],
            recv_sem=pair.at[2 * at + 1],
            device_id={"batch": 1 - bat},
            device_id_type=MESH,
        )

    cross = across(r3.at[bat], r3.at[bat], 0)
    cross.start()
    mask = own_mask(16)[None]

    def gradient(slot, block):
        d0, d1 = expand(r3, slot, block, t)
        d0 = jnp.sum(d0 * mask, axis=1, keepdims=True) * scale_i
        d1 = jnp.sum(d1 * mask, axis=1, keepdims=True) * scale_i
        return d0, d1

    def step(block, carry):
        d0, d1 = gradient(bat, block)
        w0, w1 = weight_pair(w, block)
        contract(d0 * w0 + d1 * w1, d1 * w0 - d0 * w1, ti, s4, block)
        return carry

    lax.fori_loop(0, w.shape[0] // PB, step, 0)
    send_all(n, me, *two)
    r4[me] = s4[me]
    wait_all(n, me, *small)
    summed = slots[0]
    for at in range(1, n):
        summed = summed + slots[at]
    half[bat] = summed
    other = across(half.at[bat], half.at[bat], 1)
    other.start()
    cross.wait()

    def outer(block, carry):
        at = pl.ds(block * PB, PB)
        first = None
        for slot in range(2):
            u0, u1 = expand(r1, slot, block, t)
            d0, d1 = gradient(slot, block)
            d0, d1 = d0 * (scale_f * scale_w), d1 * (scale_f * scale_w)
            real = u0 * d0 + u1 * d1
            imag = u0 * d1 - u1 * d0
            if first is None:
                first = (real, imag)
            else:
                grad[at, 0] = first[0] + real
                grad[at, 1] = first[1] + imag
        return carry

    lax.fori_loop(0, w.shape[0] // PB, outer, 0)
    other.wait()
    total[...] = half[0] + half[1]
    wait_all(n, me, *two)


def run_forward(n, scale, s1, w, t, ti):
    shape = jax.ShapeDtypeStruct
    return pl.pallas_call(
        functools.partial(mix_forward, n, scale),
        out_shape=(shape((2,) + s1.shape, BF), shape(s1.shape, BF)),
        in_specs=[VMEM] * 4,
        out_specs=(VMEM, VMEM),
        scratch_shapes=[
            pltpu.VMEM(s1.shape, BF),
            pltpu.SemaphoreType.DMA((2, 2, n)),
            pltpu.SemaphoreType.DMA((2,)),
        ],
        compiler_params=pltpu.CompilerParams(
            collective_id=0, has_side_effects=True, vmem_limit_bytes=40 << 20
        ),
        name="mix_forward",
    )(s1, w, t, ti)


def run_backward(n, scales, s3, part, w, t, ti, r1):
    shape = jax.ShapeDtypeStruct
    return pl.pallas_call(
        functools.partial(mix_backward, n, *scales),
        out_shape=(shape(w.shape, F32), shape(s3.shape, BF), shape(part.shape, F32)),
        in_specs=[VMEM] * 6,
        out_specs=(VMEM, VMEM, VMEM),
        scratch_shapes=[
            pltpu.VMEM((2,) + s3.shape, BF),
            pltpu.VMEM(s3.shape, BF),
            pltpu.VMEM((n,) + part.shape, F32),
            pltpu.VMEM((2,) + part.shape, F32),
            pltpu.SemaphoreType.DMA((3, 2, n)),
            pltpu.SemaphoreType.DMA((4,)),
        ],
        compiler_params=pltpu.CompilerParams(
            collective_id=1, has_side_effects=True, vmem_limit_bytes=48 << 20
        ),
        name="mix_backward",
    )(s3, part, w, t, ti, r1)

def half_einsum(form, left, right):
    return jnp.einsum(form, left, right, preferred_element_type=F32)


def plane_tables(rows_y, rows_z):
    phase_y = np_phase(np.arange(rows_y), np_freqs(MY, rows_y), rows_y)
    phase_z = np_phase(np.arange(rows_z), np.arange(MZ), rows_z)
    cy, sy, cz, sz = np.cos(phase_y), np.sin(phase_y), np.cos(phase_z), np.sin(phase_z)
    forward_y = np.stack([cy, -sy], axis=1)
    forward_z = np.stack([np.stack([cz, -sz], axis=1), np.stack([sz, cz], axis=1)], axis=0)
    cz, sz = cz.T, sz.T
    inverse_z = np.stack([np.stack([cz, sz], axis=1), np.stack([-sz, cz], axis=1)], axis=0)
    inverse_y = np.stack([cy.T, -sy.T], axis=0)
    return [jnp.asarray(v.astype(ml_dtypes.bfloat16)) for v in (forward_y, forward_z, inverse_z, inverse_y)]


def yz_forward(slab_data, tables):
    partial_value = half_einsum("cxyz,yrm->cxrmz", slab_data, tables[0]).astype(BF)
    return half_einsum("cxrmz,rzsk->cxsmk", partial_value, tables[1]).astype(BF)


def yz_inverse(shaped, tables, factor):
    rolled = half_einsum("oxsmk,skrz->oxrmz", shaped, tables[2]).astype(BF)
    return factor * half_einsum("oxrmz,rmy->oxyz", rolled, tables[3])


def activation_grad(pre, upstream):
    _, pull = jax.vjp(lambda values: jax.nn.gelu(values, approximate=True), pre)
    return pull(upstream)[0]


def to_send(spectrum, n):
    c, x, s, m, k = spectrum.shape
    parts = spectrum.reshape(c, x, s, n, (m * k) // n)
    return parts.transpose(3, 2, 1, 4, 0).reshape(n, s * x, (m * k) // n * c)


def from_received(received, planes, channels):
    n = received.shape[0]
    parts = received.reshape(n, 2, planes, -1, channels)
    return parts.transpose(4, 2, 1, 0, 3).reshape(channels, planes, 2, MY, MZ)


def body(field, cotangent, spectral_weight, point_weight, point_bias):
    samples, channels, planes, rows_y, rows_z = field.shape
    n = lax.axis_size("slab")
    total_samples = samples * lax.axis_size("batch")
    cells = n * planes * rows_y * rows_z
    scale_f = 1.0 / math.sqrt(cells)
    scale_i = 1.0 / math.sqrt(MX * MY * MZ)
    scale_p = 1.0 / math.sqrt(total_samples * cells)
    scale_w = math.sqrt(MX * MY * MZ / (total_samples * cells))
    tables = plane_tables(rows_y, rows_z)
    t, ti = x_tables(n, planes, channels)
    f = field[0]
    cot = cotangent[0]
    s1 = to_send(yz_forward(f, tables), n)
    r1, r2 = run_forward(n, scale_f, s1, spectral_weight, t, ti)
    back_v = from_received(r2, planes, channels)
    pre = yz_inverse(back_v, tables, scale_i) + half_einsum("ixyz,io->oxyz", f, point_weight)
    pre = pre + point_bias[:, None, None, None]
    dpre = activation_grad(pre, cot.astype(F32)).astype(BF)
    point_local = half_einsum("ixyz,oxyz->io", f, dpre)
    bias_local = jnp.sum(dpre.astype(F32), axis=(1, 2, 3))
    part = jnp.concatenate([point_local, bias_local[None], jnp.zeros((7, channels), F32)], axis=0)
    part = jnp.pad(part, ((0, 0), (0, 128 - channels)))
    s3 = to_send(yz_forward(dpre, tables), n)
    grad_spec, r4, total = run_backward(
        n, (scale_f, scale_i, scale_w), s3, part, spectral_weight, t, ti, r1
    )
    back_d = from_received(r4, planes, channels)
    input_grad = yz_inverse(back_d, tables, scale_f) + half_einsum(
        "oxyz,io->ixyz", dpre, point_weight
    )
    return (
        input_grad.astype(BF)[None],
        grad_spec,
        scale_p * total[:channels, :channels],
        scale_p * total[channels, :channels],
    )


def solution(mesh):
    placed = (
        P("batch", None, "slab", None, None),
        P("batch", None, "slab", None, None),
        P("slab", None, None, None),
        P(),
        P(),
    )
    return jax.shard_map(
        body,
        mesh=mesh,
        in_specs=placed,
        out_specs=(P("batch", None, "slab", None, None), P("slab", None, None, None), P(), P()),
        check_vma=False,
    )
```

time: 634 us -> 301 us (0.47)
  waiting for transfers between devices: 337 us -> 0 us
  Pallas kernels: 0 us -> 70.3 us
  blocking collectives: 39.7 us -> 0 us
  local copies, waits for them, and re-layouts: 110 us -> 143 us
  other arithmetic: 23.4 us -> 1.19 us
  matrix products: 99.7 us -> 80.5 us
  between operations: 14.3 us -> 0.75 us
    unnamed x7 -> x0, waiting for transfers between devices: 184 us -> none
    all_gather x2 -> x0, waiting for transfers between devices: 153 us -> none  [to_slabs(): lax.all_gather(spectrum, 'slab', axis=4, tiled=True)]
    pallas_call x0 -> x2, Pallas kernels: none -> 70.3 us  [the longest x1 39.2 us: run_backward(): pl.pallas_call(functools.partial(mix_backward, n, *scales), out_shape=(sh...]
    reshape x0 -> x10, local copies, waits for them, and re-layouts: none -> 51 us  [the longest x4 17.3 us: to_send(): parts = spectrum.reshape(c, x, s, n, m * k // n)]
    unnamed x25 -> x29, local copies, waits for them, and re-layouts: 75.7 us -> 34.1 us
    psum x1 -> x0, blocking collectives: 39.7 us -> none  [body(): lax.psum((point_local, bias_local), ('slab', 'batch'))]
    dot_general x8 -> x2, local copies, waits for them, and re-layouts: 2.27 us -> 35.4 us  [half_einsum(): return jnp.einsum(form, left, right, preferred_element_type=F32)]
    dot_general x13 -> x7, matrix products: 99.7 us -> 80.5 us  [half_einsum(): return jnp.einsum(form, left, right, preferred_element_type=F32)]
  transfers between devices with their start and end apart: 5 -> 0, of which waited for: 4 -> 0; matrix products, arithmetic and copies ran while one was open for 11% -> 0% of each run, Pallas kernels for 0% -> 0%
where the time goes in v1:
time: 301 us; the launch traced here: 296 us
  local copies, waits for them, and re-layouts  143 us (48%)
  matrix products  80.5 us (27%)
  Pallas kernels  70.3 us (23%)
    dot_general x7, matrix products, half_einsum(): return jnp.einsum(form, left, right, preferred_element_type=F32)  80.5 us
    pallas_call x1, Pallas kernels, run_backward(): pl.pallas_call(functools.partial(mix_backward, n, *scales), out_shape=(sh...  39.2 us
    dot_general x2, local copies, waits for them, and re-layouts, half_einsum(): return jnp.einsum(form, left, right, preferred_element_type=F32)  35.4 us
    unnamed x29, local copies, waits for them, and re-layouts  34.1 us
    pallas_call x1, Pallas kernels, run_forward(): pl.pallas_call(functools.partial(mix_forward, n, scale), out_shape=(shape...  31.1 us
    reshape x4, local copies, waits for them, and re-layouts, to_send(): parts = spectrum.reshape(c, x, s, n, m * k // n)  17.3 us
    reshape x2, local copies, waits for them, and re-layouts, to_send(): return parts.transpose(3, 2, 1, 4, 0).reshape(n, s * x, m * k // n * c)  16.4 us
    convert_element_type x1, local copies, waits for them, and re-layouts, body(): dpre = activation_grad(pre, cot.astype(F32)).astype(BF)  12.7 us

profile of v1, /device:TPU:0, one launch (start us, length us, event | category | flops | bytes accessed | tf_op | source)
XLA Modules:
  0.0 296.1 jit_solution(13342548207411625670)
XLA Ops:
  0.6 0.0 copy-start
  0.6 0.7 copy-done
  1.3 12.2 %fusion.18 = f32[16,8,256,128]{3,0,2,1:T(8,128)} fusion(bf16[16,8,256,128]{3,2,1,0:T(8,128)(2,1)} %bitcast.179, bf16[16,16]{1,0:T(8,128)(2,1)S(1)} %copy-done), kind=kOutput, calls=%fused_computation.27 | convolution fusion | flops 134217728 | bytes 25166336 | tf_op jit(solution)/shard_map/ixyz,io->oxyz/dot_general | solution.py:295
  13.5 0.0 copy-start.8
  13.5 0.0 copy-start.9
  13.5 17.7 %copy.32 = f32[16,8,256,128]{2,3,1,0:T(8,128)} copy(f32[16,8,256,128]{3,0,2,1:T(8,128)} %fusion.18) | data formatting | bytes 33554432 | tf_op jit(solution)/shard_map/ixyz,io->oxyz/dot_general | solution.py:295
  31.2 0.0 copy-done.8
  31.2 0.0 copy-done.9
  31.2 6.9 %fusion.37 = bf16[16,8,2,32,32]{4,3,2,1,0:T(8,128)(2,1)} fusion(bf16[2,128,2,32,1,1]{1,3,0,2,5,4:T(8,128)(2,1)S(1)} %copy-done.9, bf16[256,2,32,1,1]{0,2,1,4,3:T(8,128)(2,1)S(1)} %copy-done.8, bf16[1,16,8,256,128]{4,3,2,1,0:T(8,128)(2,1)} %param.11), kind=kOutput, calls=%fused_computation.42 | convolution fusion | flops 672399360 | bytes 8978432 | tf_op jit(solution)/shard_map/cxrmz,rzsk->cxsmk/dot_general | solution.py:295
  38.1 0.0 copy-start.1
  38.1 0.0 copy-start.2
  38.1 0.0 copy-start.7
  38.1 4.0 %reshape.37 = bf16[16,8,2,16,64]{4,3,2,1,0:T(8,128)(2,1)} reshape(bf16[16,8,2,32,32]{4,3,2,1,0:T(8,128)(2,1)} %fusion.37) | data formatting | bytes 1048576 | tf_op jit(solution)/shard_map/reshape | solution.py:327
  42.1 4.7 %copy.28 = bf16[16,8,2,16,64]{0,4,1,2,3:T(8,128)(2,1)} copy(bf16[16,8,2,16,64]{4,3,2,1,0:T(8,128)(2,1)} %reshape.37) | data formatting | bytes 1048576 | tf_op jit(solution)/shard_map/reshape | solution.py:327
  46.8 8.2 %reshape.38.s1 = bf16[16,16,1024]{2,1,0:T(8,128)(2,1)S(1)} reshape(bf16[16,2,8,64,16]{4,3,2,1,0:T(8,128)(2,1)} %bitcast.181) | data formatting | bytes 1048576 | tf_op jit(solution)/shard_map/reshape | solution.py:328
  55.0 0.0 copy-done.1
  55.0 0.0 copy-done.2
  55.0 0.0 copy-done.7
  55.0 31.1 %mix_forward.1 = (bf16[2,16,16,1024]{3,2,1,0:T(8,128)(2,1)S(1)}, bf16[16,16,1024]{2,1,0:T(8,128)(2,1)S(1)}) custom-call(bf16[16,16,1024]{2,1,0:T(8,128)(2,1)S(1)} %reshape.38.s1, bf16[64,2,16,512]{3,2,1,0:T(8,128)(2,1)S(1)} %copy-done.1, bf16[256,1024]{1,0:T(8,128)(2,1)S(1)} %copy-done.2, bf16[256,256]{1,0:T(8,128)(2,1)S(1)} %copy-done.7), custom_call_target="tpu_custom_call" | custom-call | tf_op jit(solution)/shard_map/mix_forward/pallas_call | solution.py:256
  86.1 0.0 copy-start.3
  86.1 1.1 copy-done.3
  87.2 0.0 copy-start.6
  87.2 0.8 copy-done.6
  88.0 5.4 %reshape.39 = bf16[16,2,8,64,16]{4,3,2,1,0:T(8,128)(2,1)} reshape(bf16[16,16,1024]{2,1,0:T(8,128)(2,1)} %copy-done.6) | data formatting | bytes 1048576 | tf_op jit(solution)/shard_map/reshape | solution.py:333
  93.4 5.0 %copy.29 = bf16[16,8,2,16,64]{4,3,2,1,0:T(8,128)(2,1)} copy(bf16[16,8,2,16,64]{0,4,1,2,3:T(8,128)(2,1)} %bitcast.182) | data formatting | bytes 1048576 | tf_op jit(solution)/shard_map/transpose | solution.py:334
  98.4 3.8 %reshape.51 = bf16[16,8,2,32,32,1]{4,3,2,1,0,5:T(8,128)(2,1)} reshape(bf16[16,8,2,16,64]{4,3,2,1,0:T(8,128)(2,1)} %copy.29) | data formatting | bytes 1048576 | tf_op jit(solution)/shard_map/reshape | solution.py:334
  102.2 0.0 copy-start.10
  102.2 0.0 copy-start.11
  102.2 0.0 copy-start.12
  102.2 12.3 %copy.27 = bf16[1,16,8,256,128]{3,4,2,1,0:T(8,128)(2,1)} copy(bf16[1,16,8,256,128]{4,3,2,1,0:T(8,128)(2,1)} %param.12) | data formatting | bytes 16777216 | tf_op args[1]
  114.5 0.0 copy-done.10
  114.5 0.0 copy-done.11
  114.5 0.0 copy-done.12
  114.5 21.8 %convert_reduce_fusion = (f32[16]{0:T(128)S(1)}, bf16[16,8,256,128]{2,3,1,0:T(8,128)(2,1)}) fusion(f32[16]{0:T(128)S(1)} %copy-done.12, f32[16,8,256,128]{2,3,1,0:T(8,128)} %copy.32, bf16[2,32,256,1,1]{2,1,0,4,3:T(8,128)(2,1)S(1)} %copy-done.11, bf16[2,32,2,128,1,1]{3,1,0,2,5,4:T(8,128)(2,1)S(1)} %copy-done.10, ...), kind=kOutput, calls=%fused_computation.20 | convolution fusion | flops 781189120 | bytes 34144384 | tf_op jit(solution)/shard_map/oxrmz,rmy->oxyz/dot_general | solution.py:295
  136.3 12.7 %copy.34 = bf16[16,8,256,128]{3,0,2,1:T(8,128)(2,1)} copy(bf16[16,8,256,128]{2,3,1,0:T(8,128)(2,1)} %get-tuple-element.23) | data formatting | bytes 16777216 | tf_op jit(solution)/shard_map/convert_element_type | solution.py:355
  149.0 10.6 %fusion.55 = f32[16,16]{1,0:T(8,128)S(1)} fusion(bf16[16,8,256,128]{3,0,2,1:T(8,128)(2,1)} %copy.34, bf16[16,8,256,128]{3,2,1,0:T(8,128)(2,1)} %bitcast.180), kind=kOutput, calls=%fused_computation.44 | convolution fusion | flops 134217728 | bytes 16778240 | tf_op jit(solution)/shard_map/ixyz,oxyz->io/dot_general | solution.py:295
  159.7 0.1 pad.7.clone
  159.7 0.1 maximum_maximum_fusion
  159.8 7.9 %fusion.42 = bf16[16,8,2,32,32]{4,3,2,1,0:T(8,128)(2,1)} fusion(bf16[2,128,2,32,1,1]{1,3,0,2,5,4:T(8,128)(2,1)S(1)} %copy-done.9, bf16[256,2,32,1,1]{0,2,1,4,3:T(8,128)(2,1)S(1)} %copy-done.8, bf16[16,8,256,128]{2,3,1,0:T(8,128)(2,1)} %get-tuple-element.23), kind=kOutput, calls=%fused_computation.43 | convolution fusion | flops 672399360 | bytes 8978432 | tf_op jit(solution)/shard_map/cxrmz,rzsk->cxsmk/dot_general | solution.py:295
  167.7 3.9 %reshape.41 = bf16[16,8,2,16,64]{4,3,2,1,0:T(8,128)(2,1)} reshape(bf16[16,8,2,32,32]{4,3,2,1,0:T(8,128)(2,1)} %fusion.42) | data formatting | bytes 1048576 | tf_op jit(solution)/shard_map/reshape | solution.py:327
  171.6 4.7 %copy.33 = bf16[16,8,2,16,64]{0,4,1,2,3:T(8,128)(2,1)} copy(bf16[16,8,2,16,64]{4,3,2,1,0:T(8,128)(2,1)} %reshape.41) | data formatting | bytes 1048576 | tf_op jit(solution)/shard_map/reshape | solution.py:327
  176.3 8.2 %reshape.42.s3 = bf16[16,16,1024]{2,1,0:T(8,128)(2,1)S(1)} reshape(bf16[16,2,8,64,16]{4,3,2,1,0:T(8,128)(2,1)} %bitcast.183) | data formatting | bytes 1048576 | tf_op jit(solution)/shard_map/reshape | solution.py:328
  184.5 0.0 copy-start.4
  184.5 1.2 copy-done.4
  185.7 39.2 %mix_backward.1 = (f32[64,2,16,512]{3,2,1,0:T(8,128)}, bf16[16,16,1024]{2,1,0:T(8,128)(2,1)S(1)}, f32[24,128]{1,0:T(8,128)S(1)}) custom-call(bf16[16,16,1024]{2,1,0:T(8,128)(2,1)S(1)} %reshape.42.s3, f32[24,128]{1,0:T(8,128)S(1)} %pad.4.part, bf16[64,2,16,512]{3,2,1,0:T(8,128)(2,1)S(1)} %copy-done.1, bf16[256,1024]{1,0:T(8,128)(2,1)S(1)} %copy-done.2, ...), custom_call_target="tpu_custom_call" | custom-call | tf_op jit(solution)/shard_map/mix_backward/pallas_call | solution.py:275
  224.9 0.0 copy-start.5
  225.0 0.8 copy-done.5
  225.7 5.4 %reshape.43 = bf16[16,2,8,64,16]{4,3,2,1,0:T(8,128)(2,1)} reshape(bf16[16,16,1024]{2,1,0:T(8,128)(2,1)} %copy-done.5) | data formatting | bytes 1048576 | tf_op jit(solution)/shard_map/reshape | solution.py:333
  231.2 5.0 %copy.37 = bf16[16,8,2,16,64]{4,3,2,1,0:T(8,128)(2,1)} copy(bf16[16,8,2,16,64]{0,4,1,2,3:T(8,128)(2,1)} %bitcast.184) | data formatting | bytes 1048576 | tf_op jit(solution)/shard_map/transpose | solution.py:334
  236.1 2.7 reshape.61
  238.9 11.4 %fusion.58 = f32[8,256,128,16]{2,3,1,0:T(8,128)} fusion(bf16[16,8,256,128]{3,0,2,1:T(8,128)(2,1)} %copy.34, bf16[16,16]{1,0:T(8,128)(2,1)S(1)} %copy-done), kind=kOutput, calls=%fused_computation.47 | convolution fusion | flops 134217728 | bytes 25166336 | tf_op jit(solution)/shard_map/oxyz,io->ixyz/dot_general | solution.py:295
  250.3 17.7 %copy.39 = f32[8,256,128,16]{1,2,0,3:T(8,128)} copy(f32[8,256,128,16]{2,3,1,0:T(8,128)} %fusion.58) | data formatting | bytes 33554432 | tf_op jit(solution)/shard_map/oxyz,io->ixyz/dot_general | solution.py:295
  268.0 9.7 %fusion.20 = bf16[1,16,8,256,128]{3,4,2,1,0:T(8,128)(2,1)} fusion(f32[8,256,128,16]{1,2,0,3:T(8,128)} %copy.39, bf16[2,32,256,1,1]{2,1,0,4,3:T(8,128)(2,1)S(1)} %copy-done.11, bf16[2,32,2,128,1,1]{3,1,0,2,5,4:T(8,128)(2,1)S(1)} %copy-done.10, bf16[16,8,2,32,32,1]{4,3,2,1,0,5:T(8,128)(2,1)S(1)} %reshape.61), kind=kOutput, calls=%fused_computation.29 | convolution fusion | flops 684720128 | bytes 25755648 | tf_op jit(solution)/shard_map/oxrmz,rmy->oxyz/dot_general | solution.py:295
  277.7 12.2 %copy.40 = bf16[1,16,8,256,128]{4,3,2,1,0:T(8,128)(2,1)} copy(bf16[1,16,8,256,128]{3,4,2,1,0:T(8,128)(2,1)} %fusion.20) | data formatting | bytes 16777216
  290.0 0.6 slice_multiply_fusion
  290.6 0.5 multiply_bitcast_fusion
  291.1 5.0 %copy.69 = f32[64,2,16,512]{3,2,1,0:T(8,128)} copy(f32[64,2,16,512]{3,2,1,0:T(8,128)} %get-tuple-element.29) | data formatting | bytes 8388608
  (2 shorter events, 0.0 us)
Async XLA Ops:
  0.6 0.7 copy-start
  13.5 17.7 %copy-start.8 = (bf16[256,2,32,1,1]{0,2,1,4,3:T(8,128)(2,1)S(1)}, bf16[256,2,32,1,1]{0,2,1,4,3:T(8,128)(2,1)}, u32[]{:S(2)}) copy-start(bf16[256,2,32,1,1]{0,2,1,4,3:T(8,128)(2,1)} %constant.47) | copy-start | bytes 98308
  13.5 17.7 %copy-start.9 = (bf16[2,128,2,32,1,1]{1,3,0,2,5,4:T(8,128)(2,1)S(1)}, bf16[2,128,2,32,1,1]{1,3,0,2,5,4:T(8,128)(2,1)}, u32[]{:S(2)}) copy-start(bf16[2,128,2,32,1,1]{1,3,0,2,5,4:T(8,128)(2,1)} %constant.48) | copy-start | bytes 98308
  38.1 16.9 %copy-start.1 = (bf16[64,2,16,512]{3,2,1,0:T(8,128)(2,1)S(1)}, bf16[64,2,16,512]{3,2,1,0:T(8,128)(2,1)}, u32[]{:S(2)}) copy-start(bf16[64,2,16,512]{3,2,1,0:T(8,128)(2,1)} %w.3) | copy-start | bytes 6291460
  38.1 16.9 %copy-start.2 = (bf16[256,1024]{1,0:T(8,128)(2,1)S(1)}, bf16[256,1024]{1,0:T(8,128)(2,1)}, u32[]{:S(2)}) copy-start(bf16[256,1024]{1,0:T(8,128)(2,1)} %constant.40.clone.t) | copy-start | bytes 1572868
  38.1 16.9 %copy-start.7 = (bf16[256,256]{1,0:T(8,128)(2,1)S(1)}, bf16[256,256]{1,0:T(8,128)(2,1)}, u32[]{:S(2)}) copy-start(bf16[256,256]{1,0:T(8,128)(2,1)} %constant.41.clone.ti) | copy-start | bytes 393220
  86.1 1.1 copy-start.3
  87.2 0.8 copy-start.6
  102.2 12.3 %copy-start.10 = (bf16[2,32,2,128,1,1]{3,1,0,2,5,4:T(8,128)(2,1)S(1)}, bf16[2,32,2,128,1,1]{3,1,0,2,5,4:T(8,128)(2,1)}, u32[]{:S(2)}) copy-start(bf16[2,32,2,128,1,1]{3,1,0,2,5,4:T(8,128)(2,1)} %constant.50) | copy-start | bytes 98308
  102.2 12.3 %copy-start.11 = (bf16[2,32,256,1,1]{2,1,0,4,3:T(8,128)(2,1)S(1)}, bf16[2,32,256,1,1]{2,1,0,4,3:T(8,128)(2,1)}, u32[]{:S(2)}) copy-start(bf16[2,32,256,1,1]{2,1,0,4,3:T(8,128)(2,1)} %constant.51) | copy-start | bytes 98308
  102.2 12.3 %copy-start.12 = (f32[16]{0:T(128)S(1)}, f32[16]{0:T(128)}, u32[]{:S(2)}) copy-start(f32[16]{0:T(128)} %param.15) | copy-start | bytes 196
  184.5 1.2 copy-start.4
  224.9 0.8 copy-start.5
